TPU v7x, 512 devices: a whole 4x4x16 slice. The times are simulated.
512 devices in a mesh: body: 2 (over core), gx: 16 (over z), gy: 16 (over x, y).
Axes of the slice: x: 4, y: 4, z: 16, core: 2. Of those that a mesh axis runs over, the one named last changes fastest.
Arguments:
- disp: float32 [2, 3, 128, 512, 128], P('body', None, 'gx', 'gy'), may hold values from -4 to 4
- force: float32 [2, 3, 128, 512, 128], P('body', None, 'gx', 'gy'), may hold values from -12 to 12
- kappa: float32 [2, 128, 512, 128], P('body', 'gx', 'gy'), may hold values from 0.05 to 0.5
- sigma: float32 [2, 128, 512, 128], P('body', 'gx', 'gy'), may hold values from 0.2 to 1
- gap0: float32 [512, 128], P(('gx', 'gy')), may hold values from -3 to 3
- pressure: float32 [512, 128], P(('gx', 'gy')), may hold values from 0 to 1
- mortar: float32 [512, 128, 128], P(('gx', 'gy')), may hold values from -0.5 to 0.5
- partner: int32 [512], P(('gx', 'gy')), may hold values from 0 to 31
- active: int32 [512], P(('gx', 'gy')), may hold values 0 or 1
Outputs:
- increment: float32 [2, 3, 128, 512, 128], P('body', None, 'gx', 'gy')
- new_pressure: float32 [512, 128], P(('gx', 'gy'))
Inputs may be any that keep to these rules, and one draw needn't show every extreme that they name: partner numbers a master block of the same gy index: gx index times 2 plus the local block. 1 marks a block of the active contact set.
All inputs are finite; a program needn't handle non-finite values.
Results may differ from a plain program's by a relative error of at most 0.00015.
Values sent between devices are 32-bit elements; how exact they have to be, the bound alone decides.
No kernel may reach another device: no remote copies, remote signals or barrier semaphores. Data moves between devices by JAX's collectives and lax.ppermute only.
A program may use at most 64 MiB of HBM per device.

v0:
```python
import jax
import jax.numpy as jnp
from jax import lax
from jax.sharding import PartitionSpec as P

SBLK = 128
CG_ITERS = 2


def extended(block, sides, width):
    for axis, dim in sides:
        count = lax.axis_size(axis)
        forward = [(i, i + 1) for i in range(count - 1)]
        backward = [(target, source) for source, target in forward]
        low = lax.ppermute(
            lax.slice_in_dim(block, block.shape[dim] - width, None, axis=dim), axis, forward
        )
        high = lax.ppermute(lax.slice_in_dim(block, 0, width, axis=dim), axis, backward)
        block = jnp.concatenate([low, block, high], axis=dim)
    return block


def neighbours():
    result = []
    for first in (-1, 0, 1):
        for second in (-1, 0, 1):
            for third in (-1, 0, 1):
                if first != 0 or second != 0 or third != 0:
                    result.append((first, second, third))
    return result


def apply_stencil(field, padded, kappa, kappa_rim, sigma):
    sizes = field.shape[2:]
    total = sigma[:, None] * field
    for offset in neighbours():
        weight = 0.5 ** (abs(offset[0]) + abs(offset[1]) + abs(offset[2]) - 1)
        lower = [1 + offset[0], 1 + offset[1], 1 + offset[2]]
        bond = 0.5 * (
            kappa
            + kappa_rim[
                :,
                lower[0] : lower[0] + sizes[0],
                lower[1] : lower[1] + sizes[1],
                lower[2] : lower[2] + sizes[2],
            ]
        )
        near = padded[
            :,
            :,
            lower[0] : lower[0] + sizes[0],
            lower[1] : lower[1] + sizes[1],
            lower[2] : lower[2] + sizes[2],
        ]
        total = total + weight * bond[:, None] * (field - near)
    return total


def stencil(field, kappa, kappa_rim, sigma):
    padded = extended(field, (("gx", 2), ("gy", 3)), 1)
    padded = jnp.pad(padded, ((0, 0), (0, 0), (0, 0), (0, 0), (1, 1)))
    return apply_stencil(field, padded, kappa, kappa_rim, sigma)


def gap_of(field, selector, mortar):
    own = field[0, 2, :, :, 0].reshape(1, -1, SBLK)
    rows = lax.all_gather(own, ("body", "gx"), axis=0, tiled=True)
    row_count = lax.axis_size("gx")
    slave_own = lax.dynamic_index_in_dim(rows, lax.axis_index("gx"), 0, keepdims=False)
    master_row = rows[row_count:].reshape(-1, SBLK)
    picked = jnp.dot(selector, master_row, precision=lax.Precision.HIGHEST)
    pulled = jnp.einsum("bij,bj->bi", mortar, picked, precision=lax.Precision.HIGHEST)
    return -slave_own - pulled


def spread(traction, selector, mortar):
    pulled = jnp.einsum("bij,bi->bj", mortar, traction, precision=lax.Precision.HIGHEST)
    row_terms = -jnp.dot(selector.T, pulled, precision=lax.Precision.HIGHEST)
    share = lax.psum_scatter(row_terms, "gx", scatter_dimension=0, tiled=True)
    return jnp.where(lax.axis_index("body") == 0, -traction, share)


def add_surface(image, surface):
    return image.at[0, 2, :, :, 0].add(surface.reshape(image.shape[2], image.shape[3]))


def global_sum(value):
    return lax.psum(value, ("body", "gx", "gy"))


def on_device(disp, force, kappa, sigma, gap0, pressure, mortar, partner, active):
    kappa_rim = extended(kappa, (("gx", 1), ("gy", 2)), 1)
    kappa_rim = jnp.pad(kappa_rim, ((0, 0), (0, 0), (0, 0), (1, 1)))
    row_blocks = mortar.shape[0] * lax.axis_size("gx")
    selector = (partner[:, None] == jnp.arange(row_blocks, dtype=jnp.int32)[None, :]).astype(
        jnp.float32
    )
    flags = active.astype(jnp.float32)[:, None]
    gap = gap0 + gap_of(disp, selector, mortar)
    radius = jnp.sqrt(gap * gap + pressure * pressure + 0.01)
    complement = gap + pressure - radius
    slope_gap = 1.0 - gap / radius
    slope_press = 1.0 - pressure / radius
    divisor = slope_press + 0.5
    stiffness = flags * slope_gap / divisor
    excess = flags * complement / divisor
    rhs = force - stencil(disp, kappa, kappa_rim, sigma)
    rhs = add_surface(rhs, spread(flags * pressure - excess, selector, mortar))
    increment = jnp.zeros_like(rhs)
    residual = rhs
    direction = rhs
    norm_now = global_sum(jnp.sum(residual * residual))
    for step in range(CG_ITERS):
        image = stencil(direction, kappa, kappa_rim, sigma)
        image = add_surface(
            image, spread(stiffness * gap_of(direction, selector, mortar), selector, mortar)
        )
        alpha = norm_now / lax.psum(jnp.sum(direction * image), ("body", "gx", "gy"))
        increment = increment + alpha * direction
        residual = residual - alpha * image
        norm_next = global_sum(jnp.sum(residual * residual))
        direction = residual + norm_next / norm_now * direction
        norm_now = norm_next
    change = gap_of(increment, selector, mortar)
    new_press = flags * (pressure - (complement + slope_gap * change) / divisor)
    return (increment, new_press)


def solution(mesh):
    placed = (
        P("body", None, "gx", "gy", None),
        P("body", None, "gx", "gy", None),
        P("body", "gx", "gy", None),
        P("body", "gx", "gy", None),
        P(("gx", "gy"), None),
        P(("gx", "gy"), None),
        P(("gx", "gy"), None, None),
        P(("gx", "gy")),
        P(("gx", "gy")),
    )
    return jax.shard_map(
        on_device,
        mesh=mesh,
        in_specs=placed,
        out_specs=(P("body", None, "gx", "gy", None), P(("gx", "gy"), None)),
        check_vma=False,
    )
```

profile of v0, /device:TPU:1, one launch (start us, length us, event | category | flops | bytes accessed | tf_op | source)
XLA Modules:
  0.0 782.8 jit_solution(5270657747271295689)
XLA Ops:
  1.5 4.4 collective-permute-start.4
  5.9 1.3 collective-permute-start.5
  7.9 4.2 collective-permute-start
  12.1 1.3 collective-permute-start.1
  13.4 1.0 slice_reduce_fusion.2
  15.2 61.1 %all_gather.12 = f32[32,2,128]{2,1,0:T(2,128)S(1)} all-gather(f32[1,2,128]{2,1,0:T(2,128)S(1)} %reshape_squeeze.12), channel_id=1, replica_groups=mesh['body'=2,'gx'=16,'gy'=16] {'body','gx'}, dimensions={0}, use_global_device_ids=true | all-gather | bytes 33792 | tf_op jit(solution)/shard_map/all_gather | solution.py:67
  79.3 1.3 dynamic-slice.22
  81.3 39.8 %all-reduce.4 = f32[32,128]{1,0:T(8,128)S(1)} all-reduce(f32[32,128]{1,0:T(8,128)S(1)} %convolution_negate_fusion.2), channel_id=2, replica_groups=mesh['body'=2,'gx'=16,'gy'=16] {'gx'}, use_global_device_ids=true, to_apply=%region_0.1.clone | all-reduce | flops 4096 | bytes 32768
  122.0 1.3 collective-permute-start.3
  123.3 4.0 collective-permute-start.2
  129.4 1.3 collective-permute-start.7
  130.7 4.2 collective-permute-start.6
  136.5 2.3 fusion.16
  139.1 1.3 collective-permute-start.9
  140.4 4.0 collective-permute-start.8
  144.5 70.0 %all_gather.13 = f32[32,2,128]{2,1,0:T(2,128)S(1)} all-gather(f32[1,2,128]{2,1,0:T(2,128)S(1)} %reshape_squeeze.13), channel_id=1, replica_groups=mesh['body'=2,'gx'=16,'gy'=16] {'body','gx'}, dimensions={0}, use_global_device_ids=true | all-gather | bytes 33792 | tf_op jit(solution)/shard_map/all_gather | solution.py:67
  216.2 39.1 %all-reduce.5 = f32[32,128]{1,0:T(8,128)S(1)} all-reduce(f32[32,128]{1,0:T(8,128)S(1)} %convolution_negate_fusion.1), channel_id=3, replica_groups=mesh['body'=2,'gx'=16,'gy'=16] {'gx'}, use_global_device_ids=true, to_apply=%region_3.4.clone | all-reduce | flops 4096 | bytes 32768
  255.3 1.3 collective-permute-start.11
  256.6 4.5 collective-permute-start.10
  263.8 2.9 fusion.95
  267.7 125.8 %all-reduce.7 = (f32[]{:T(128)}, f32[]{:T(128)}) all-reduce(f32[]{:T(128)} %get-tuple-element.39, f32[]{:T(128)} %get-tuple-element.38), channel_id=1, replica_groups=mesh['body'=2,'gx'=16,'gy'=16] {'body','gx','gy'}, use_global_device_ids=true, to_apply=%region_2.3 | all-reduce | flops 2 | bytes 16 | tf_op jit(solution)/shard_map/psum | solution.py:88
  395.5 99.7 %psum.30 = f32[]{:T(128)} all-reduce(f32[]{:T(128)} %multiply_reduce_fusion.1), channel_id=1, replica_groups=mesh['body'=2,'gx'=16,'gy'=16] {'body','gx','gy'}, use_global_device_ids=true, to_apply=%region_7.8 | all-reduce | flops 1 | bytes 8 | tf_op jit(solution)/shard_map/psum | solution.py:88
  496.7 1.3 collective-permute-start.13
  498.0 4.0 collective-permute-start.12
  502.1 52.8 %all_gather.14 = f32[32,2,128]{2,1,0:T(2,128)S(1)} all-gather(f32[1,2,128]{2,1,0:T(2,128)S(1)} %reshape_squeeze.14), channel_id=1, replica_groups=mesh['body'=2,'gx'=16,'gy'=16] {'body','gx'}, dimensions={0}, use_global_device_ids=true | all-gather | bytes 33792 | tf_op jit(solution)/shard_map/all_gather | solution.py:67
  557.0 0.9 convolution_negate_fusion
  557.9 39.2 %all-reduce.6 = f32[32,128]{1,0:T(8,128)S(1)} all-reduce(f32[32,128]{1,0:T(8,128)S(1)} %convolution_negate_fusion), channel_id=4, replica_groups=mesh['body'=2,'gx'=16,'gy'=16] {'gx'}, use_global_device_ids=true, to_apply=%region_8.9.clone | all-reduce | flops 4096 | bytes 32768
  597.1 1.3 collective-permute-start.15
  598.4 4.2 collective-permute-start.14
  605.4 2.9 fusion.41
  609.2 117.7 %psum.31 = f32[]{:T(128)} all-reduce(f32[]{:T(128)} %multiply_reduce_fusion), channel_id=1, replica_groups=mesh['body'=2,'gx'=16,'gy'=16] {'body','gx','gy'}, use_global_device_ids=true, to_apply=%region_10.11 | all-reduce | flops 1 | bytes 8 | tf_op jit(solution)/shard_map/psum | solution.py:118
  728.5 53.1 %all_gather.15 = f32[32,2,128]{2,1,0:T(2,128)S(1)} all-gather(f32[1,2,128]{2,1,0:T(2,128)S(1)} %reshape_squeeze.15), channel_id=1, replica_groups=mesh['body'=2,'gx'=16,'gy'=16] {'body','gx'}, dimensions={0}, use_global_device_ids=true | all-gather | bytes 33792 | tf_op jit(solution)/shard_map/all_gather | solution.py:67
  (165 shorter events, 23.4 us)
Async XLA Ops:
  0.6 76.5 %copy-start = (f32[2,128,128]{2,1,0:T(8,128)S(1)}, f32[2,128,128]{2,1,0:T(8,128)}, u32[]{:S(2)}) copy-start(f32[2,128,128]{2,1,0:T(8,128)} %param.21) | copy-start | bytes 393220
  0.6 127.6 %copy-start.26 = (f32[1,8,32,128]{3,2,1,0:T(8,128)S(1)}, f32[1,8,32,128]{3,2,1,0:T(8,128)}, u32[]{:S(2)}) copy-start(f32[1,8,32,128]{3,2,1,0:T(8,128)} %param.17) | copy-start | bytes 393220
  1.5 127.2 %collective-permute-start.4 = (f32[1,3,1,32,128]{4,3,2,1,0:T(8,128)S(1)}, f32[1,3,1,32,128]{4,3,2,1,0:T(8,128)S(1)}, u32[]{:S(2)}, u32[]{:S(2)}) collective-permute-start(f32[1,3,1,32,128]{4,3,2,1,0:T(8,128)S(1)} %get-tuple-element.82), channel_id=1, source_target_pairs={{0,16},{16,32},{32,48},{48,64},{64,80},{80,96},{96,112},{112,128},... | collective-permute-start | bytes 147464 | tf_op jit(solution)/shard_map/ppermute | solution.py:15
  5.9 123.4 %collective-permute-start.5 = (f32[1,3,1,32,128]{4,3,2,1,0:T(8,128)S(1)}, f32[1,3,1,32,128]{4,3,2,1,0:T(8,128)S(1)}, u32[]{:S(2)}, u32[]{:S(2)}) collective-permute-start(f32[1,3,1,32,128]{4,3,2,1,0:T(8,128)S(1)} %get-tuple-element.81), channel_id=1, source_target_pairs={{16,0},{32,16},{48,32},{64,48},{80,64},{96,80},{112,96},{128,112},... | collective-permute-start | bytes 147464 | tf_op jit(solution)/shard_map/ppermute | solution.py:18
  7.9 113.1 %collective-permute-start = (f32[1,1,32,128]{3,2,1,0:T(8,128)S(1)}, f32[1,1,32,128]{3,2,1,0:T(8,128)S(1)}, u32[]{:S(2)}, u32[]{:S(2)}) collective-permute-start(f32[1,1,32,128]{3,2,1,0:T(8,128)S(1)} %get-tuple-element.97), channel_id=1, source_target_pairs={{0,16},{16,32},{32,48},{48,64},{64,80},{80,96},{96,112},{112,128},... | collective-permute-start | bytes 49160 | tf_op jit(solution)/shard_map/ppermute | solution.py:15
  12.1 109.8 %collective-permute-start.1 = (f32[1,1,32,128]{3,2,1,0:T(8,128)S(1)}, f32[1,1,32,128]{3,2,1,0:T(8,128)S(1)}, u32[]{:S(2)}, u32[]{:S(2)}) collective-permute-start(f32[1,1,32,128]{3,2,1,0:T(8,128)S(1)} %get-tuple-element.96), channel_id=1, source_target_pairs={{16,0},{32,16},{48,32},{64,48},{80,64},{96,80},{112,96},{128,112},... | collective-permute-start | bytes 49160 | tf_op jit(solution)/shard_map/ppermute | solution.py:18
  122.0 5.5 collective-permute-start.3
  123.3 4.7 collective-permute-start.2
  128.8 134.0 %copy-start.2 = (f32[8,32,128]{2,1,0:T(8,128)}, f32[8,32,128]{2,1,0:T(8,128)S(1)}, u32[]{:S(2)}) copy-start(f32[8,32,128]{2,1,0:T(8,128)S(1)} %get-tuple-element.66) | copy-start | bytes 393220
  129.4 5.8 collective-permute-start.7
  130.7 5.1 collective-permute-start.6
  135.0 3.8 copy-start.8
  135.0 3.8 copy-start.11
  135.1 3.7 copy-start.14
  135.1 127.6 %copy-start.4 = (f32[8,32,128]{2,1,0:T(8,128)}, f32[8,32,128]{2,1,0:T(8,128)S(1)}, u32[]{:S(2)}) copy-start(f32[8,32,128]{2,1,0:T(8,128)S(1)} %get-tuple-element.83) | copy-start | bytes 393220
  135.1 127.6 %copy-start.6 = (f32[8,32,128]{2,1,0:T(8,128)}, f32[8,32,128]{2,1,0:T(8,128)S(1)}, u32[]{:S(2)}) copy-start(f32[8,32,128]{2,1,0:T(8,128)S(1)} %get-tuple-element.84) | copy-start | bytes 393220
  136.5 78.0 %copy-start.39 = (s32[2]{0:T(128)S(1)}, s32[2]{0:T(128)}, u32[]{:S(2)}) copy-start(s32[2]{0:T(128)} %param.22) | copy-start | bytes 28
  136.5 78.5 %copy-start.38 = (f32[2,128]{1,0:T(2,128)S(1)}, f32[2,128]{1,0:T(2,128)}, u32[]{:S(2)}) copy-start(f32[2,128]{1,0:T(2,128)} %param.20) | copy-start | bytes 3076
  139.1 116.1 %collective-permute-start.9 = (f32[1,3,1,32,128]{4,3,2,1,0:T(8,128)S(1)}, f32[1,3,1,32,128]{4,3,2,1,0:T(8,128)S(1)}, u32[]{:S(2)}, u32[]{:S(2)}) collective-permute-start(f32[1,3,1,32,128]{4,3,2,1,0:T(8,128)S(1)} %get-tuple-element.80), channel_id=1, source_target_pairs={{16,0},{32,16},{48,32},{64,48},{80,64},{96,80},{112,96},{128,112},... | collective-permute-start | bytes 147464 | tf_op jit(solution)/shard_map/ppermute | solution.py:18
  140.4 114.8 %collective-permute-start.8 = (f32[1,3,1,32,128]{4,3,2,1,0:T(8,128)S(1)}, f32[1,3,1,32,128]{4,3,2,1,0:T(8,128)S(1)}, u32[]{:S(2)}, u32[]{:S(2)}) collective-permute-start(f32[1,3,1,32,128]{4,3,2,1,0:T(8,128)S(1)} %get-tuple-element.79), channel_id=1, source_target_pairs={{0,16},{16,32},{32,48},{48,64},{64,80},{80,96},{96,112},{112,128},... | collective-permute-start | bytes 147464 | tf_op jit(solution)/shard_map/ppermute | solution.py:15
  255.2 7.5 copy-start.32
  255.2 7.5 copy-start.33
  255.3 6.7 collective-permute-start.11
  256.6 5.4 collective-permute-start.10
  496.7 100.4 %collective-permute-start.13 = (f32[1,3,1,32,128]{4,3,2,1,0:T(8,128)S(1)}, f32[1,3,1,32,128]{4,3,2,1,0:T(8,128)S(1)}, u32[]{:S(2)}, u32[]{:S(2)}) collective-permute-start(f32[1,3,1,32,128]{4,3,2,1,0:T(8,128)S(1)} %get-tuple-element.78), channel_id=1, source_target_pairs={{16,0},{32,16},{48,32},{64,48},{80,64},{96,80},{112,96},{128,112},... | collective-permute-start | bytes 147464 | tf_op jit(solution)/shard_map/ppermute | solution.py:18
  498.0 99.1 %collective-permute-start.12 = (f32[1,3,1,32,128]{4,3,2,1,0:T(8,128)S(1)}, f32[1,3,1,32,128]{4,3,2,1,0:T(8,128)S(1)}, u32[]{:S(2)}, u32[]{:S(2)}) collective-permute-start(f32[1,3,1,32,128]{4,3,2,1,0:T(8,128)S(1)} %get-tuple-element.77), channel_id=1, source_target_pairs={{0,16},{16,32},{32,48},{48,64},{64,80},{80,96},{96,112},{112,128},... | collective-permute-start | bytes 147464 | tf_op jit(solution)/shard_map/ppermute | solution.py:15
  597.1 7.1 copy-start.30
  597.1 7.1 copy-start.31
  597.1 6.4 collective-permute-start.15
  598.4 5.1 collective-permute-start.14
  608.3 173.3 %copy-start.40 = (s32[2]{0:T(128)S(1)}, s32[2]{0:T(128)}, u32[]{:S(2)}) copy-start(s32[2]{0:T(128)} %param.22) | copy-start | bytes 28
  728.3 54.5 %copy-start.34 = (f32[1,3,8,32,128]{4,3,2,1,0:T(8,128)}, f32[1,3,8,32,128]{4,3,2,1,0:T(8,128)S(1)}, u32[]{:S(2)}) copy-start(f32[1,3,8,32,128]{4,3,2,1,0:T(8,128)S(1)} %multiply_add_fusion) | copy-start | bytes 1179652
  (25 other events, 39.2 us)
where the time goes:
time: 784 us; the launch traced here: 783 us
  blocking collectives  698 us (89%)
  starting transfers between devices  43.8 us (6%)
  other arithmetic  16.7 us (2%)
  local copies, waits for them, and re-layouts  10.8 us (1%)
    all_gather x4, blocking collectives, gap_of(): rows = lax.all_gather(own, ('body', 'gx'), axis=0, tiled=True)  237 us
    psum x2, blocking collectives, global_sum(): return lax.psum(value, ('body', 'gx', 'gy'))  226 us
    unnamed x3, blocking collectives  118 us
    psum x1, blocking collectives, on_device(): lax.psum(jnp.sum(direction * image), ('body', 'gx', 'gy'))  118 us
    ppermute x8, starting transfers between devices, extended(): lax.ppermute(lax.slice_in_dim(block, block.shape[dim] - width, None, axis...  33.4 us
  transfers between devices with their start and end apart: 16, of which 2 were waited for; matrix products, arithmetic and copies ran while one was open for 2% of the time, Pallas kernels for 0%

commit v1 on v0

--- a/solution.py
+++ b/solution.py
@@ -85,7 +85,7 @@
 
 
 def global_sum(value):
-    return lax.psum(value, ("body", "gx", "gy"))
+    return lax.psum(lax.psum(value, "body"), ("gx", "gy"))
 
 
 def on_device(disp, force, kappa, sigma, gap0, pressure, mortar, partner, active):

time: 784 us -> 2060 us (2.63)
  blocking collectives: 698 us -> 1970 us
    psum x2 -> x4, blocking collectives: 226 us -> 1180 us  [global_sum(): return lax.psum(lax.psum(value, 'body'), ('gx', 'gy'))]
    psum x1 -> x2, blocking collectives: 118 us -> 323 us  [on_device(): lax.psum(jnp.sum(direction * image), ('body', 'gx', 'gy'))]
    all_gather x4, blocking collectives: 237 us -> 345 us  [gap_of(): rows = lax.all_gather(own, ('body', 'gx'), axis=0, tiled=True)]
  transfers between devices with their start and end apart: 16 -> 16, of which waited for: 2 -> 2; matrix products, arithmetic and copies ran while one was open for 2% -> 1% of each run, Pallas kernels for 0% -> 0%
where the time goes in v1:
time: 2060 us; the launch traced here: 2050 us
  blocking collectives  1970 us (96%)
  starting transfers between devices  43.8 us (2%)
    psum x4, blocking collectives, global_sum(): return lax.psum(lax.psum(value, 'body'), ('gx', 'gy'))  1180 us
    all_gather x4, blocking collectives, gap_of(): rows = lax.all_gather(own, ('body', 'gx'), axis=0, tiled=True)  345 us
    psum x2, blocking collectives, on_device(): lax.psum(jnp.sum(direction * image), ('body', 'gx', 'gy'))  323 us
    unnamed x3, blocking collectives  118 us
  transfers between devices with their start and end apart: 16, of which 2 were waited for; matrix products, arithmetic and copies ran while one was open for 1% of the time, Pallas kernels for 0%

profile of v1, /device:TPU:1, one launch (start us, length us, event | category | flops | bytes accessed | tf_op | source)
XLA Modules:
  0.0 2054.1 jit_solution(18371233217776994178)
XLA Ops:
  1.5 4.4 collective-permute-start.4
  5.9 1.3 collective-permute-start.5
  7.9 4.2 collective-permute-start
  12.1 1.3 collective-permute-start.1
  15.2 61.1 %all_gather.12 = f32[32,2,128]{2,1,0:T(2,128)S(1)} all-gather(f32[1,2,128]{2,1,0:T(2,128)S(1)} %reshape_squeeze.12), channel_id=1, replica_groups=mesh['body'=2,'gx'=16,'gy'=16] {'body','gx'}, dimensions={0}, use_global_device_ids=true | all-gather | bytes 33792 | tf_op jit(solution)/shard_map/all_gather | solution.py:67
  81.3 39.8 %all-reduce.4 = f32[32,128]{1,0:T(8,128)S(1)} all-reduce(f32[32,128]{1,0:T(8,128)S(1)} %convolution_negate_fusion.2), channel_id=2, replica_groups=mesh['body'=2,'gx'=16,'gy'=16] {'gx'}, use_global_device_ids=true, to_apply=%region_0.1.clone | all-reduce | flops 4096 | bytes 32768
  122.0 1.3 collective-permute-start.3
  123.3 4.0 collective-permute-start.2
  129.4 1.3 collective-permute-start.7
  130.7 4.2 collective-permute-start.6
  136.5 2.3 fusion.16
  139.1 1.3 collective-permute-start.9
  140.4 4.0 collective-permute-start.8
  144.5 70.0 %all_gather.13 = f32[32,2,128]{2,1,0:T(2,128)S(1)} all-gather(f32[1,2,128]{2,1,0:T(2,128)S(1)} %reshape_squeeze.13), channel_id=1, replica_groups=mesh['body'=2,'gx'=16,'gy'=16] {'body','gx'}, dimensions={0}, use_global_device_ids=true | all-gather | bytes 33792 | tf_op jit(solution)/shard_map/all_gather | solution.py:67
  216.2 39.1 %all-reduce.5 = f32[32,128]{1,0:T(8,128)S(1)} all-reduce(f32[32,128]{1,0:T(8,128)S(1)} %convolution_negate_fusion.1), channel_id=3, replica_groups=mesh['body'=2,'gx'=16,'gy'=16] {'gx'}, use_global_device_ids=true, to_apply=%region_4.5.clone | all-reduce | flops 4096 | bytes 32768
  255.3 1.3 collective-permute-start.11
  256.6 4.5 collective-permute-start.10
  263.8 2.9 fusion.95
  267.7 19.8 psum.42
  287.5 583.1 %psum.43 = f32[]{:T(128)} all-reduce(f32[]{:T(128)} %psum.42), channel_id=1, replica_groups=mesh['body'=2,'gx'=16,'gy'=16] {'gx','gy'}, use_global_device_ids=true, to_apply=%region_3.4 | all-reduce | flops 1 | bytes 8 | tf_op jit(solution)/shard_map/psum | solution.py:88
  870.6 207.2 %psum.44 = f32[]{:T(128)} all-reduce(f32[]{:T(128)} %get-tuple-element.38), channel_id=1, replica_groups=mesh['body'=2,'gx'=16,'gy'=16] {'body','gx','gy'}, use_global_device_ids=true, to_apply=%region_6.7 | all-reduce | flops 1 | bytes 8 | tf_op jit(solution)/shard_map/psum | solution.py:118
  1080.0 3.4 psum.45
  1083.4 577.4 %psum.46 = f32[]{:T(128)} all-reduce(f32[]{:T(128)} %psum.45), channel_id=1, replica_groups=mesh['body'=2,'gx'=16,'gy'=16] {'gx','gy'}, use_global_device_ids=true, to_apply=%region_9.10 | all-reduce | flops 1 | bytes 8 | tf_op jit(solution)/shard_map/psum | solution.py:88
  1662.4 1.3 collective-permute-start.13
  1663.7 4.0 collective-permute-start.12
  1667.7 161.0 %all_gather.14 = f32[32,2,128]{2,1,0:T(2,128)S(1)} all-gather(f32[1,2,128]{2,1,0:T(2,128)S(1)} %reshape_squeeze.14), channel_id=1, replica_groups=mesh['body'=2,'gx'=16,'gy'=16] {'body','gx'}, dimensions={0}, use_global_device_ids=true | all-gather | bytes 33792 | tf_op jit(solution)/shard_map/all_gather | solution.py:67
  1831.7 39.1 %all-reduce.6 = f32[32,128]{1,0:T(8,128)S(1)} all-reduce(f32[32,128]{1,0:T(8,128)S(1)} %convolution_negate_fusion), channel_id=4, replica_groups=mesh['body'=2,'gx'=16,'gy'=16] {'gx'}, use_global_device_ids=true, to_apply=%region_10.11.clone | all-reduce | flops 4096 | bytes 32768
  1870.8 1.3 collective-permute-start.15
  1872.1 4.2 collective-permute-start.14
  1879.1 2.9 fusion.41
  1882.9 115.8 %psum.47 = f32[]{:T(128)} all-reduce(f32[]{:T(128)} %multiply_reduce_fusion), channel_id=1, replica_groups=mesh['body'=2,'gx'=16,'gy'=16] {'body','gx','gy'}, use_global_device_ids=true, to_apply=%region_12.13 | all-reduce | flops 1 | bytes 8 | tf_op jit(solution)/shard_map/psum | solution.py:118
  2000.3 52.6 %all_gather.15 = f32[32,2,128]{2,1,0:T(2,128)S(1)} all-gather(f32[1,2,128]{2,1,0:T(2,128)S(1)} %reshape_squeeze.15), channel_id=1, replica_groups=mesh['body'=2,'gx'=16,'gy'=16] {'body','gx'}, dimensions={0}, use_global_device_ids=true | all-gather | bytes 33792 | tf_op jit(solution)/shard_map/all_gather | solution.py:67
  (168 shorter events, 26.7 us)
Async XLA Ops:
  0.6 76.5 %copy-start = (f32[2,128,128]{2,1,0:T(8,128)S(1)}, f32[2,128,128]{2,1,0:T(8,128)}, u32[]{:S(2)}) copy-start(f32[2,128,128]{2,1,0:T(8,128)} %param.21) | copy-start | bytes 393220
  0.6 127.6 %copy-start.26 = (f32[1,8,32,128]{3,2,1,0:T(8,128)S(1)}, f32[1,8,32,128]{3,2,1,0:T(8,128)}, u32[]{:S(2)}) copy-start(f32[1,8,32,128]{3,2,1,0:T(8,128)} %param.17) | copy-start | bytes 393220
  1.5 127.2 %collective-permute-start.4 = (f32[1,3,1,32,128]{4,3,2,1,0:T(8,128)S(1)}, f32[1,3,1,32,128]{4,3,2,1,0:T(8,128)S(1)}, u32[]{:S(2)}, u32[]{:S(2)}) collective-permute-start(f32[1,3,1,32,128]{4,3,2,1,0:T(8,128)S(1)} %get-tuple-element.80), channel_id=1, source_target_pairs={{0,16},{16,32},{32,48},{48,64},{64,80},{80,96},{96,112},{112,128},... | collective-permute-start | bytes 147464 | tf_op jit(solution)/shard_map/ppermute | solution.py:15
  5.9 123.4 %collective-permute-start.5 = (f32[1,3,1,32,128]{4,3,2,1,0:T(8,128)S(1)}, f32[1,3,1,32,128]{4,3,2,1,0:T(8,128)S(1)}, u32[]{:S(2)}, u32[]{:S(2)}) collective-permute-start(f32[1,3,1,32,128]{4,3,2,1,0:T(8,128)S(1)} %get-tuple-element.79), channel_id=1, source_target_pairs={{16,0},{32,16},{48,32},{64,48},{80,64},{96,80},{112,96},{128,112},... | collective-permute-start | bytes 147464 | tf_op jit(solution)/shard_map/ppermute | solution.py:18
  7.9 113.1 %collective-permute-start = (f32[1,1,32,128]{3,2,1,0:T(8,128)S(1)}, f32[1,1,32,128]{3,2,1,0:T(8,128)S(1)}, u32[]{:S(2)}, u32[]{:S(2)}) collective-permute-start(f32[1,1,32,128]{3,2,1,0:T(8,128)S(1)} %get-tuple-element.95), channel_id=1, source_target_pairs={{0,16},{16,32},{32,48},{48,64},{64,80},{80,96},{96,112},{112,128},... | collective-permute-start | bytes 49160 | tf_op jit(solution)/shard_map/ppermute | solution.py:15
  12.1 109.8 %collective-permute-start.1 = (f32[1,1,32,128]{3,2,1,0:T(8,128)S(1)}, f32[1,1,32,128]{3,2,1,0:T(8,128)S(1)}, u32[]{:S(2)}, u32[]{:S(2)}) collective-permute-start(f32[1,1,32,128]{3,2,1,0:T(8,128)S(1)} %get-tuple-element.94), channel_id=1, source_target_pairs={{16,0},{32,16},{48,32},{64,48},{80,64},{96,80},{112,96},{128,112},... | collective-permute-start | bytes 49160 | tf_op jit(solution)/shard_map/ppermute | solution.py:18
  122.0 5.5 collective-permute-start.3
  123.3 4.7 collective-permute-start.2
  128.8 134.0 %copy-start.2 = (f32[8,32,128]{2,1,0:T(8,128)}, f32[8,32,128]{2,1,0:T(8,128)S(1)}, u32[]{:S(2)}) copy-start(f32[8,32,128]{2,1,0:T(8,128)S(1)} %get-tuple-element.64) | copy-start | bytes 393220
  129.4 5.8 collective-permute-start.7
  130.7 5.1 collective-permute-start.6
  135.0 3.8 copy-start.8
  135.0 3.8 copy-start.11
  135.1 3.7 copy-start.14
  135.1 127.7 %copy-start.4 = (f32[8,32,128]{2,1,0:T(8,128)}, f32[8,32,128]{2,1,0:T(8,128)S(1)}, u32[]{:S(2)}) copy-start(f32[8,32,128]{2,1,0:T(8,128)S(1)} %get-tuple-element.81) | copy-start | bytes 393220
  135.1 127.7 %copy-start.6 = (f32[8,32,128]{2,1,0:T(8,128)}, f32[8,32,128]{2,1,0:T(8,128)S(1)}, u32[]{:S(2)}) copy-start(f32[8,32,128]{2,1,0:T(8,128)S(1)} %get-tuple-element.82) | copy-start | bytes 393220
  136.5 78.0 %copy-start.39 = (s32[2]{0:T(128)S(1)}, s32[2]{0:T(128)}, u32[]{:S(2)}) copy-start(s32[2]{0:T(128)} %param.22) | copy-start | bytes 28
  136.5 78.5 %copy-start.38 = (f32[2,128]{1,0:T(2,128)S(1)}, f32[2,128]{1,0:T(2,128)}, u32[]{:S(2)}) copy-start(f32[2,128]{1,0:T(2,128)} %param.20) | copy-start | bytes 3076
  139.1 116.1 %collective-permute-start.9 = (f32[1,3,1,32,128]{4,3,2,1,0:T(8,128)S(1)}, f32[1,3,1,32,128]{4,3,2,1,0:T(8,128)S(1)}, u32[]{:S(2)}, u32[]{:S(2)}) collective-permute-start(f32[1,3,1,32,128]{4,3,2,1,0:T(8,128)S(1)} %get-tuple-element.78), channel_id=1, source_target_pairs={{16,0},{32,16},{48,32},{64,48},{80,64},{96,80},{112,96},{128,112},... | collective-permute-start | bytes 147464 | tf_op jit(solution)/shard_map/ppermute | solution.py:18
  140.4 114.8 %collective-permute-start.8 = (f32[1,3,1,32,128]{4,3,2,1,0:T(8,128)S(1)}, f32[1,3,1,32,128]{4,3,2,1,0:T(8,128)S(1)}, u32[]{:S(2)}, u32[]{:S(2)}) collective-permute-start(f32[1,3,1,32,128]{4,3,2,1,0:T(8,128)S(1)} %get-tuple-element.77), channel_id=1, source_target_pairs={{0,16},{16,32},{32,48},{48,64},{64,80},{80,96},{96,112},{112,128},... | collective-permute-start | bytes 147464 | tf_op jit(solution)/shard_map/ppermute | solution.py:15
  255.2 7.5 copy-start.32
  255.2 7.5 copy-start.33
  255.3 6.7 collective-permute-start.11
  256.6 5.4 collective-permute-start.10
  1662.4 208.4 %collective-permute-start.13 = (f32[1,3,1,32,128]{4,3,2,1,0:T(8,128)S(1)}, f32[1,3,1,32,128]{4,3,2,1,0:T(8,128)S(1)}, u32[]{:S(2)}, u32[]{:S(2)}) collective-permute-start(f32[1,3,1,32,128]{4,3,2,1,0:T(8,128)S(1)} %get-tuple-element.76), channel_id=1, source_target_pairs={{16,0},{32,16},{48,32},{64,48},{80,64},{96,80},{112,96},{128,112},... | collective-permute-start | bytes 147464 | tf_op jit(solution)/shard_map/ppermute | solution.py:18
  1663.7 207.1 %collective-permute-start.12 = (f32[1,3,1,32,128]{4,3,2,1,0:T(8,128)S(1)}, f32[1,3,1,32,128]{4,3,2,1,0:T(8,128)S(1)}, u32[]{:S(2)}, u32[]{:S(2)}) collective-permute-start(f32[1,3,1,32,128]{4,3,2,1,0:T(8,128)S(1)} %get-tuple-element.75), channel_id=1, source_target_pairs={{0,16},{16,32},{32,48},{48,64},{64,80},{80,96},{96,112},{112,128},... | collective-permute-start | bytes 147464 | tf_op jit(solution)/shard_map/ppermute | solution.py:15
  1870.8 7.1 copy-start.30
  1870.8 7.1 copy-start.31
  1870.8 6.4 collective-permute-start.15
  1872.1 5.1 collective-permute-start.14
  1882.1 170.9 %copy-start.40 = (s32[2]{0:T(128)S(1)}, s32[2]{0:T(128)}, u32[]{:S(2)}) copy-start(s32[2]{0:T(128)} %param.22) | copy-start | bytes 28
  2000.1 53.9 %copy-start.34 = (f32[1,3,8,32,128]{4,3,2,1,0:T(8,128)}, f32[1,3,8,32,128]{4,3,2,1,0:T(8,128)S(1)}, u32[]{:S(2)}) copy-start(f32[1,3,8,32,128]{4,3,2,1,0:T(8,128)S(1)} %multiply_add_fusion) | copy-start | bytes 1179652
  (25 other events, 39.2 us)
